TPU v7x, 32 devices: a whole 2x2x4 slice. The times are simulated.
32 devices in a mesh: group: 8 (over z, y), member: 4 (over x, core).
Axes of the slice: x: 2, y: 2, z: 4, core: 2. Of those that a mesh axis runs over, the one named last changes fastest.
Arguments:
- points: float32 [32, 8, 1024], P(('group', 'member')), may hold values from -4 to 4
- inverse_cov: bfloat16 [32, 1024, 1024], P(('group', 'member')), may hold values from -1 to 4, as said below
- targets: bfloat16 [32, 1024], P(('group', 'member')), may hold values from -6 to 6
- queries: float32 [8, 2048], P(None, ('group', 'member')), may hold values from -4 to 4
- prior_precision: float32 [2048], P(('group', 'member')), may hold values from 0.05 to 0.2
- batch_order: int32 [2048], replicated, may hold values from 0 to 2047, each once
- noise: float32 [2048, 1024], P('group', 'member'), may hold values from -6 to 6
Outputs:
- samples: float32 [2048, 1024], P('group', 'member')
Inputs may be any that keep to these rules, and one draw needn't show every extreme that they name: `batch_order`: each query number appears exactly once. `inverse_cov`: each expert's matrix is symmetric positive definite.
All inputs are finite; a program needn't handle non-finite values.
Results may differ from a plain program's by a relative error of at most 0.0025.
Values sent between devices are 32-bit elements; how exact they have to be, the bound alone decides.
A program may use at most 128 MiB of HBM per device.

v0:
```python
import functools

import jax
import jax.numpy as jnp
from jax import lax
from jax.experimental import pallas as pl
from jax.experimental.pallas import tpu as pltpu
from jax.sharding import PartitionSpec as P

kernel_rate = 0.25
f32, bf16 = jnp.float32, jnp.bfloat16
LEAF = 16
MESH = pl.DeviceIdType.MESH
VMEM_LIMIT = 48 * 1024 * 1024


def split3(x):
    high = x.astype(bf16)
    rest = x - high.astype(f32)
    mid = rest.astype(bf16)
    low = (rest - mid.astype(f32)).astype(bf16)
    return high, mid, low


def iota(shape, dim):
    return lax.broadcasted_iota(jnp.int32, shape, dim)


def dot_rows(a, b):
    return lax.dot_general(a, b, (((0,), (0,)), ((), ())), preferred_element_type=f32)


def dot_lanes(a, b):
    return lax.dot_general(a, b, (((1,), (1,)), ((), ())), preferred_element_type=f32)


def select(groups, members, wide, order, shift, rows):
    share = wide.shape[1] // 3
    per = share // 2
    owner = lax.shift_right_logical(order, per.bit_length() - 1)
    place = (order & (per - 1)) + shift
    onehot = jnp.where(iota((share, order.shape[1]), 0) == place, 1.0, 0.0).astype(bf16)
    found = jnp.dot(wide, jnp.concatenate([onehot] * 3, axis=0), preferred_element_type=f32)
    total = jnp.zeros((rows, order.shape[1]), f32)
    for m in range(members):
        for g in range(groups):
            at = (m * groups + g) * 8
            total = total + jnp.where(owner == g * members + m, found[at : at + rows], 0.0)
    return total


def terms_kernel(
    groups,
    members,
    batch,
    queries_ref,
    prior_ref,
    order_ref,
    points_ref,
    inverse_hbm,
    targets_ref,
    out_ref,
    sorted_ref,
    own,
    gathered,
    table,
    inverse,
    point_rows,
    cross,
    proj,
    packed,
    from_core,
    pair_sum,
    from_x,
    chip_sum,
    from_y,
    line_sum,
    from_z,
    piece,
    whole,
    load_sem,
    row_send,
    row_recv,
    block_send,
    block_recv,
    core_send,
    core_recv,
    x_send,
    x_recv,
    y_send,
    y_recv,
    z_send,
    z_recv,
    last_send,
    last_recv,
):
    g, m = lax.axis_index("group"), lax.axis_index("member")
    far, near = groups // 2, members // 2
    gz, gy = g // 2, g % 2
    mx, mc = m // 2, m % 2
    half = batch // 2
    chunk = 2 * batch
    share = batch // members

    load = pltpu.make_async_copy(inverse_hbm, inverse, load_sem)
    load.start()

    def other_group(k):
        return lax.rem(g + k, groups), m

    def other_member(k):
        return g, lax.rem(m + k, members)

    def line_peer(k):
        return lax.rem(gz + k, far) * 2 + gy, m

    y_peer = (g + 1 - 2 * gy, m)
    core_peer = (g, m + 1 - 2 * mc)

    barrier = pltpu.get_barrier_semaphore()
    for k in range(1, groups):
        pl.semaphore_signal(barrier, inc=1, device_id=other_group(k), device_id_type=MESH)
    for k in range(1, members):
        pl.semaphore_signal(barrier, inc=1, device_id=other_member(k), device_id_type=MESH)

    per = queries_ref.shape[1]
    own[...] = jnp.concatenate(
        [queries_ref[...], jnp.broadcast_to(prior_ref[...], (8, per))], axis=1
    )
    pl.semaphore_wait(barrier, groups + members - 2)

    def remote(src, dst, send, recv, device):
        return pltpu.make_async_remote_copy(
            src_ref=src, dst_ref=dst, send_sem=send, recv_sem=recv, device_id=device, device_id_type=MESH
        )

    rows_out = [
        remote(own, gathered.at[m, g], row_send.at[k - 1], row_recv.at[k - 1], other_group(k)) for k in range(1, groups)
    ]
    for copy in rows_out:
        copy.start()
    gathered[m, g] = own[...]

    coords = points_ref[...]
    count = coords.shape[1]
    p1, p2, p3 = split3(coords)
    n1, n2, n3 = split3(-kernel_rate * jnp.sum(coords * coords, axis=0, keepdims=True))
    ones = jnp.ones((1, count), bf16)
    none = jnp.zeros((10, count), bf16)
    point_rows[...] = jnp.concatenate([p1, p2, p1, p2, p3, p1, n1, n2, n3, ones, ones, ones, none], axis=0)
    row, col = iota((half, half), 0), iota((half, half), 1)
    values = jnp.broadcast_to(targets_ref[...].astype(f32), (16, count)).astype(bf16)

    for copy in rows_out:
        copy.wait_recv()
    blocks_out = [
        remote(gathered.at[m], gathered.at[m], block_send.at[k - 1], block_recv.at[k - 1], other_member(k))
        for k in range(1, members)
    ]
    for copy in blocks_out:
        copy.start()
    for copy in blocks_out:
        copy.wait_recv()
    for e in range(members):
        tiles = gathered[e].reshape(groups * 8, own.shape[1])
        table[e * groups * 8 : (e + 1) * groups * 8, :] = jnp.concatenate(split3(tiles), axis=1)

    def core_copy(s):
        return remote(packed.at[s, 1 - mc], from_core.at[s], core_send.at[s], core_recv.at[s], core_peer)

    def x_copy(s, k):
        peer = lax.rem(mx + k, near)
        return remote(
            pair_sum.at[s, peer], from_x.at[s, k - 1], x_send.at[s, k - 1], x_recv.at[s, k - 1], (g, peer * 2 + mc)
        )

    def y_copy(s):
        return remote(chip_sum.at[s, 1 - gy], from_y.at[s], y_send.at[s], y_recv.at[s], y_peer)

    def z_copy(s):
        return remote(line_sum.at[s], from_z.at[s], z_send.at[s], z_recv.at[s], line_peer(s + 1))

    def after_core(s):
        core_copy(s).wait_recv()
        pair_sum[s] = packed[s, mc] + from_core[s]
        for k in range(1, near):
            x_copy(s, k).start()

    def after_x(s):
        total = pair_sum[s, mx]
        for k in range(1, near):
            x_copy(s, k).wait_recv()
            total = total + from_x[s, k - 1]
        chip_sum[s] = total
        y_copy(s).start()

    def after_y(s):
        y_copy(s).wait_recv()
        line_sum[s] = chip_sum[s, gy] + from_y[s]

    def step(s, _):
        pair = lax.rem(gz + 1 + s, far)
        order = order_ref[:, pl.ds(pl.multiple_of(pair * chunk, chunk), chunk)]
        q = select(groups, members, table[...], order, 0, 8)
        m1, m2, m3 = split3(-kernel_rate * jnp.sum(q * q, axis=0, keepdims=True))
        s1, s2, s3 = split3(2.0 * kernel_rate * q)
        one = jnp.ones((1, chunk), bf16)
        zero = jnp.zeros((10, chunk), bf16)
        query_rows = jnp.concatenate([s1, s1, s2, s2, s1, s3, one, one, one, m1, m2, m3, zero], axis=0)
        cross[...] = jnp.exp(dot_rows(query_rows, point_rows[...])).astype(bf16)

        @pl.when(s >= 1)
        def _():
            after_core(s - 1)

        @pl.when(s == 0)
        def _():
            load.wait()

        proj[...] = jnp.dot(cross[...], inverse[...], preferred_element_type=f32).astype(bf16)

        @pl.when(s >= 1)
        def _():
            after_x(s - 1)

        info = dot_lanes(values, proj[...])
        for b in range(2):
            rows = slice(b * batch, (b + 1) * batch)
            left = jnp.concatenate([proj[rows, :], cross[rows, :]], axis=1)
            right = jnp.concatenate([cross[rows, :], proj[rows, :]], axis=1)
            term = 0.5 * dot_lanes(left, right)
            first, second = term[:half, :half], term[half:, half:]
            main = jnp.concatenate([jnp.where(row >= col, first, second), term[half:, :half]], axis=0)
            diagonal = jnp.sum(jnp.where(row == col, second, 0.0), axis=0, keepdims=True)
            line = info[0:1, rows]
            more = jnp.concatenate([diagonal, line[:, :half], line[:, half:], jnp.zeros((5, half), f32)], axis=0)
            for e in range(members):
                packed[s, e % 2, e // 2, b, 0:share, :] = main[e * share : (e + 1) * share]
                packed[s, e % 2, e // 2, b, share : share + 8, :] = more if e == 0 else jnp.zeros_like(more)
        core_copy(s).start()

        @pl.when(s >= 1)
        def _():
            after_y(s - 1)
            z_copy(s - 1).start()

        return 0

    lax.fori_loop(0, far, step, 0)
    last = far - 1
    after_core(last)
    mine = order_ref[:, pl.ds(pl.multiple_of(g * batch, batch), batch)]
    sorted_ref[...] = select(groups, members, table[...], mine, per, 1)
    after_x(last)
    after_y(last)
    total = line_sum[last]
    for s in range(last):
        z_copy(s).wait_recv()
        total = total + from_z[s]
    piece[...] = total
    pieces_out = [
        remote(piece, whole.at[m], last_send.at[k - 1], last_recv.at[k - 1], other_member(k)) for k in range(1, members)
    ]
    for copy in pieces_out:
        copy.start()
    whole[m] = total
    for copy in rows_out + blocks_out:
        copy.wait_send()
    for s in range(far):
        core_copy(s).wait_send()
        for k in range(1, near):
            x_copy(s, k).wait_send()
        y_copy(s).wait_send()
        if s < last:
            z_copy(s).wait_send()
    for copy in pieces_out:
        copy.wait_recv()
    out_ref[...] = whole[...]
    for copy in pieces_out:
        copy.wait_send()


def factor_kernel(experts, packed_ref, prior_ref, noise_hbm, out_ref, noise, work, inverse, forward, load_sem):
    load = pltpu.make_async_copy(noise_hbm, noise, load_sem)
    load.start()
    batch = noise.shape[0]
    half = batch // 2
    members, share = packed_ref.shape[0], packed_ref.shape[1] - 8
    main = jnp.concatenate([packed_ref[e, 0:share, :] for e in range(members)], axis=0)
    scale = 1.0 / experts
    row, col = iota((half, half), 0), iota((half, half), 1)
    mixed = main[:half] * scale
    lower = jnp.where(row >= col, mixed, 0.0)
    upper = jnp.where(row < col, mixed, 0.0)
    below = main[half:] * scale
    tail = packed_ref[0, share : share + 8, :] * scale
    prior = prior_ref[...]
    first = lower + jnp.where(row < col, lower.T, 0.0)
    first = first + jnp.where(row == col, prior[:, :half], 0.0)
    second = upper + upper.T + jnp.where(row == col, tail[0:1] + prior[:, half:], 0.0)
    work[0:half, 0:half] = first
    work[0:half, half:batch] = below.T
    work[half:batch, 0:half] = below
    work[half:batch, half:batch] = second
    work[0:half, batch:] = jnp.broadcast_to(tail[1:2], (half, half)).T
    work[half:batch, batch:] = jnp.broadcast_to(tail[2:3], (half, half)).T

    width = batch + half
    sub = iota((LEAF, half), 0)
    wide_sub, lane = iota((LEAF, width), 0), iota((LEAF, width), 1)
    for start in range(0, batch, LEAF):
        stop = start + LEAF
        rows = work[start:stop, :]
        cols = [jnp.broadcast_to(rows[:, start + k : start + k + 1], (LEAF, half)) for k in range(LEAF)]
        rows = jnp.where((lane >= start) & (lane < stop), jnp.where(lane - start == wide_sub, 1.0, 0.0), rows)
        pivots = jnp.ones((LEAF, half), f32)
        for j in range(LEAF):
            pivot = jnp.broadcast_to(cols[j][j : j + 1], (LEAF, half))
            pivots = jnp.where(sub == j, pivot, pivots)
            if j + 1 < LEAF:
                factor = jnp.where(sub > j, cols[j] * (1.0 / pivot), 0.0)
                for k in range(j + 1, LEAF):
                    cols[k] = cols[k] - factor * cols[k][j : j + 1]
                rows = rows - jnp.concatenate([factor] * 3, axis=1) * rows[j : j + 1]
        rows = rows * jnp.concatenate([lax.rsqrt(pivots)] * 3, axis=1)
        inverse[start:stop, :] = jnp.where(lane < stop, rows, 0.0)[:, :batch]
        forward[start:stop, :] = rows[:, batch:]
        if stop < batch:
            base = stop // half * half
            a1, a2, a3 = split3(rows)
            right = jnp.concatenate([a1, a2, a1, a2, a3, a1], axis=0)
            left = jnp.concatenate([a1, a1, a2, a2, a1, a3], axis=0)[:, base:batch]
            update = dot_rows(left, right)[stop - base :]
            rest = work[stop:batch, :]
            inside = iota(rest.shape, 1)
            rest = jnp.where((inside >= start) & (inside < stop), 0.0, rest)
            work[stop:batch, :] = rest - update

    load.wait()
    side = noise[...] + jnp.concatenate([forward[...]] * 2, axis=1)
    out_ref[...] = lax.dot_general(
        inverse[...], side, (((0,), (0,)), ((), ())), precision=lax.Precision.HIGHEST, preferred_element_type=f32
    )


def in_vmem(count):
    return [pl.BlockSpec(memory_space=pltpu.VMEM)] * count


def per_device(points, inverse_cov, targets, queries, prior_precision, batch_order, noise):
    batch = noise.shape[0]
    groups = lax.axis_size("group")
    members = lax.axis_size("member")
    experts = points.shape[0] * groups * members
    half = batch // 2
    far, near = groups // 2, members // 2
    size = batch // members + 8
    dim, count = points.shape[1:]
    vmem, dma = pltpu.VMEM, pltpu.SemaphoreType.DMA
    packed, prior_batch = pl.pallas_call(
        functools.partial(terms_kernel, groups, members, batch),
        out_shape=(
            jax.ShapeDtypeStruct((members, size, half), f32),
            jax.ShapeDtypeStruct((1, batch), f32),
        ),
        in_specs=in_vmem(4) + [pl.BlockSpec(memory_space=pl.ANY)] + in_vmem(1),
        out_specs=tuple(in_vmem(2)),
        scratch_shapes=[
            vmem((dim, 2 * queries.shape[1]), f32),
            vmem((members, groups, dim, 2 * queries.shape[1]), f32),
            vmem((members * groups * dim, 6 * queries.shape[1]), bf16),
            vmem((count, count), bf16),
            vmem((64, count), bf16),
            vmem((2 * batch, count), bf16),
            vmem((2 * batch, count), bf16),
            vmem((far, 2, near, 2, size, half), f32),
            vmem((far, near, 2, size, half), f32),
            vmem((far, near, 2, size, half), f32),
            vmem((far, near - 1, 2, size, half), f32),
            vmem((far, 2, size, half), f32),
            vmem((far, size, half), f32),
            vmem((far, size, half), f32),
            vmem((far - 1, size, half), f32),
            vmem((size, half), f32),
            vmem((members, size, half), f32),
            dma,
            dma((groups - 1,)),
            dma((groups - 1,)),
            dma((members - 1,)),
            dma((members - 1,)),
            dma((far,)),
            dma((far,)),
            dma((far, near - 1)),
            dma((far, near - 1)),
            dma((far,)),
            dma((far,)),
            dma((far - 1,)),
            dma((far - 1,)),
            dma((members - 1,)),
            dma((members - 1,)),
        ],
        compiler_params=pltpu.CompilerParams(vmem_limit_bytes=VMEM_LIMIT, collective_id=0, has_side_effects=True),
        name="terms",
    )(queries, prior_precision[None, :], batch_order[None, :], points[0], inverse_cov[0], targets)
    return pl.pallas_call(
        functools.partial(factor_kernel, experts),
        out_shape=jax.ShapeDtypeStruct(noise.shape, f32),
        in_specs=in_vmem(2) + [pl.BlockSpec(memory_space=pl.ANY)],
        out_specs=pl.BlockSpec(memory_space=vmem),
        scratch_shapes=[
            vmem(noise.shape, f32),
            vmem((batch, batch + half), f32),
            vmem((batch, batch), f32),
            vmem((batch, half), f32),
            dma,
        ],
        compiler_params=pltpu.CompilerParams(vmem_limit_bytes=VMEM_LIMIT),
        name="factor",
    )(packed, prior_batch, noise)


def solution(mesh):
    return jax.shard_map(
        per_device,
        mesh=mesh,
        in_specs=(
            P(("group", "member"), None, None),
            P(("group", "member"), None, None),
            P(("group", "member"), None),
            P(None, ("group", "member")),
            P(("group", "member")),
            P(),
            P("group", "member"),
        ),
        out_specs=P("group", "member"),
        check_vma=False,
    )
```

profile of v0, /device:TPU:0, one launch (start us, length us, event | category | flops | bytes accessed | tf_op | source)
XLA Modules:
  0.0 61.0 jit_solution(13020498167493397985)
XLA Ops:
  0.0 0.0 copy-start
  0.0 1.6 %copy-done = bf16[1,1024,1024]{2,1,0:T(8,128)(2,1)S(1)} copy-done((bf16[1,1024,1024]{2,1,0:T(8,128)(2,1)S(1)}, bf16[1,1024,1024]{2,1,0:T(8,128)(2,1)}, u32[]{:S(2)}) %copy-start) | copy-done | bytes 2097176
  1.6 0.0 copy-start.2
  1.6 0.8 %copy-done.2 = f32[1,8,1024]{2,1,0:T(8,128)S(1)} copy-done((f32[1,8,1024]{2,1,0:T(8,128)S(1)}, f32[1,8,1024]{2,1,0:T(8,128)}, u32[]{:S(2)}) %copy-start.2) | copy-done | bytes 32792
  2.4 0.0 copy-start.3
  2.4 0.7 %copy-done.3 = s32[2048]{0:T(1024)S(1)} copy-done((s32[2048]{0:T(1024)S(1)}, s32[2048]{0:T(1024)}, u32[]{:S(2)}) %copy-start.3) | copy-done | bytes 8216
  3.0 0.0 copy-start.4
  3.0 0.7 %copy-done.4 = f32[8,64]{1,0:T(8,128)S(1)} copy-done((f32[8,64]{1,0:T(8,128)S(1)}, f32[8,64]{1,0:T(8,128)}, u32[]{:S(2)}) %copy-start.4) | copy-done | bytes 2072
  3.7 0.0 copy-start.5
  3.7 0.7 %copy-done.5 = bf16[1,1024]{1,0:T(2,128)(2,1)S(1)} copy-done((bf16[1,1024]{1,0:T(2,128)(2,1)S(1)}, bf16[1,1024]{1,0:T(2,128)(2,1)}, u32[]{:S(2)}) %copy-start.5) | copy-done | bytes 2072
  4.4 0.0 copy-start.6
  4.4 0.7 %copy-done.6 = f32[64]{0:T(128)S(1)} copy-done((f32[64]{0:T(128)S(1)}, f32[64]{0:T(128)}, u32[]{:S(2)}) %copy-start.6) | copy-done | bytes 280
  5.1 0.0 copy-start.1
  5.1 47.1 %terms.1 = (f32[4,72,128]{2,1,0:T(8,128)S(1)}, f32[1,256]{1,0:T(1,128)S(1)}) custom-call(f32[8,64]{1,0:T(8,128)S(1)} %copy-done.4, f32[1,64]{1,0:T(1,128)S(1)} %bitcast.7, s32[1,2048]{1,0:T(1,128)S(1)} %bitcast.6, f32[8,1024]{1,0:T(8,128)S(1)} %bitcast.5, bf16[1024,1024]{1,0:T(8,128)(2,1)S(1)} %bitcast.4, bf16[1,1024]{1,0:T(2,128)(2,1)S(1)} %copy-done.5), custom_call_target="tpu_custom_call" | custom-call | tf_op jit(solution)/shard_map/terms/pallas_call | solution.py:360
  52.2 0.0 copy-done.1
  52.2 8.8 %factor.1 = f32[256,256]{1,0:T(8,128)} custom-call(f32[4,72,128]{2,1,0:T(8,128)S(1)} %get-tuple-element.7.packed_ref, f32[1,256]{1,0:T(1,128)S(1)} %get-tuple-element.8.prior_ref, f32[256,256]{1,0:T(8,128)S(1)} %copy-done.1), custom_call_target="tpu_custom_call" | custom-call | tf_op jit(solution)/shard_map/factor/pallas_call | solution.py:405
Async XLA Ops:
  0.0 1.6 %copy-start = (bf16[1,1024,1024]{2,1,0:T(8,128)(2,1)S(1)}, bf16[1,1024,1024]{2,1,0:T(8,128)(2,1)}, u32[]{:S(2)}) copy-start(bf16[1,1024,1024]{2,1,0:T(8,128)(2,1)} %param.8) | copy-start | bytes 6291460
  1.6 0.8 %copy-start.2 = (f32[1,8,1024]{2,1,0:T(8,128)S(1)}, f32[1,8,1024]{2,1,0:T(8,128)}, u32[]{:S(2)}) copy-start(f32[1,8,1024]{2,1,0:T(8,128)} %param.7) | copy-start | bytes 98308
  2.4 0.7 %copy-start.3 = (s32[2048]{0:T(1024)S(1)}, s32[2048]{0:T(1024)}, u32[]{:S(2)}) copy-start(s32[2048]{0:T(1024)} %param.12) | copy-start | bytes 24580
  3.0 0.7 %copy-start.4 = (f32[8,64]{1,0:T(8,128)S(1)}, f32[8,64]{1,0:T(8,128)}, u32[]{:S(2)}) copy-start(f32[8,64]{1,0:T(8,128)} %queries_ref.1) | copy-start | bytes 6148
  3.7 0.7 %copy-start.5 = (bf16[1,1024]{1,0:T(2,128)(2,1)S(1)}, bf16[1,1024]{1,0:T(2,128)(2,1)}, u32[]{:S(2)}) copy-start(bf16[1,1024]{1,0:T(2,128)(2,1)} %targets_ref.1) | copy-start | bytes 6148
  4.4 0.7 %copy-start.6 = (f32[64]{0:T(128)S(1)}, f32[64]{0:T(128)}, u32[]{:S(2)}) copy-start(f32[64]{0:T(128)} %param.11) | copy-start | bytes 772
  5.1 47.1 %copy-start.1 = (f32[256,256]{1,0:T(8,128)S(1)}, f32[256,256]{1,0:T(8,128)}, u32[]{:S(2)}) copy-start(f32[256,256]{1,0:T(8,128)} %noise_hbm.1) | copy-start | bytes 786436
where the time goes:
time: 61.3 us; the launch traced here: 61 us
  Pallas kernels  55.9 us (91%)
  local copies, waits for them, and re-layouts  5.08 us (8%)
    pallas_call x1, Pallas kernels, per_device(): pl.pallas_call(functools.partial(terms_kernel, groups, members, batch), o...  47.1 us
    pallas_call x1, Pallas kernels, per_device(): pl.pallas_call(functools.partial(factor_kernel, experts), out_shape=jax.S...  8.83 us
    unnamed x14, local copies, waits for them, and re-layouts  5.08 us

commit v1 on v0

--- a/solution.py
+++ b/solution.py
@@ -11,7 +11,7 @@
 f32, bf16 = jnp.float32, jnp.bfloat16
 LEAF = 16
 MESH = pl.DeviceIdType.MESH
-VMEM_LIMIT = 48 * 1024 * 1024
+VMEM_LIMIT = 63 * 1024 * 1024
 
 
 def split3(x):
@@ -53,14 +53,19 @@
     groups,
     members,
     batch,
+    queries_hbm,
+    prior_hbm,
+    order_hbm,
+    points_hbm,
+    inverse_hbm,
+    targets_hbm,
+    out_ref,
+    sorted_ref,
     queries_ref,
     prior_ref,
     order_ref,
     points_ref,
-    inverse_hbm,
     targets_ref,
-    out_ref,
-    sorted_ref,
     own,
     gathered,
     table,
@@ -71,24 +76,20 @@
     packed,
     from_core,
     pair_sum,
-    from_x,
-    chip_sum,
-    from_y,
+    from_xy,
     line_sum,
     from_z,
     piece,
     whole,
-    load_sem,
+    load_sems,
     row_send,
     row_recv,
     block_send,
     block_recv,
     core_send,
     core_recv,
-    x_send,
-    x_recv,
-    y_send,
-    y_recv,
+    xy_send,
+    xy_recv,
     z_send,
     z_recv,
     last_send,
@@ -102,8 +103,11 @@
     chunk = 2 * batch
     share = batch // members
 
-    load = pltpu.make_async_copy(inverse_hbm, inverse, load_sem)
-    load.start()
+    sources = (queries_hbm, prior_hbm, points_hbm.at[0], order_hbm, targets_hbm, inverse_hbm.at[0])
+    places = (queries_ref, prior_ref, points_ref, order_ref, targets_ref, inverse)
+    loads = [pltpu.make_async_copy(a, b, load_sems.at[i]) for i, (a, b) in enumerate(zip(sources, places))]
+    for load in loads:
+        load.start()
 
     def other_group(k):
         return lax.rem(g + k, groups), m
@@ -114,7 +118,6 @@
     def line_peer(k):
         return lax.rem(gz + k, far) * 2 + gy, m
 
-    y_peer = (g + 1 - 2 * gy, m)
     core_peer = (g, m + 1 - 2 * mc)
 
     barrier = pltpu.get_barrier_semaphore()
@@ -124,6 +127,8 @@
         pl.semaphore_signal(barrier, inc=1, device_id=other_member(k), device_id_type=MESH)
 
     per = queries_ref.shape[1]
+    for load in loads[:2]:
+        load.wait()
     own[...] = jnp.concatenate(
         [queries_ref[...], jnp.broadcast_to(prior_ref[...], (8, per))], axis=1
     )
@@ -141,6 +146,8 @@
         copy.start()
     gathered[m, g] = own[...]
 
+    for load in loads[2:5]:
+        load.wait()
     coords = points_ref[...]
     count = coords.shape[1]
     p1, p2, p3 = split3(coords)
@@ -168,14 +175,20 @@
     def core_copy(s):
         return remote(packed.at[s, 1 - mc], from_core.at[s], core_send.at[s], core_recv.at[s], core_peer)
 
-    def x_copy(s, k):
-        peer = lax.rem(mx + k, near)
-        return remote(
-            pair_sum.at[s, peer], from_x.at[s, k - 1], x_send.at[s, k - 1], x_recv.at[s, k - 1], (g, peer * 2 + mc)
-        )
-
-    def y_copy(s):
-        return remote(chip_sum.at[s, 1 - gy], from_y.at[s], y_send.at[s], y_recv.at[s], y_peer)
+    def xy_copies(s):
+        copies = []
+        for k in range(1, 2 * near):
+            peer, to = lax.rem(mx + k // 2, near), lax.rem(gy + k % 2, 2)
+            copies.append(
+                remote(
+                    pair_sum.at[s, peer, to],
+                    from_xy.at[s, k - 1],
+                    xy_send.at[s, k - 1],
+                    xy_recv.at[s, k - 1],
+                    (gz * 2 + to, peer * 2 + mc),
+                )
+            )
+        return copies
 
     def z_copy(s):
         return remote(line_sum.at[s], from_z.at[s], z_send.at[s], z_recv.at[s], line_peer(s + 1))
@@ -183,20 +196,15 @@
     def after_core(s):
         core_copy(s).wait_recv()
         pair_sum[s] = packed[s, mc] + from_core[s]
-        for k in range(1, near):
-            x_copy(s, k).start()
-
-    def after_x(s):
-        total = pair_sum[s, mx]
-        for k in range(1, near):
-            x_copy(s, k).wait_recv()
-            total = total + from_x[s, k - 1]
-        chip_sum[s] = total
-        y_copy(s).start()
-
-    def after_y(s):
-        y_copy(s).wait_recv()
-        line_sum[s] = chip_sum[s, gy] + from_y[s]
+        for copy in xy_copies(s):
+            copy.start()
+
+    def after_xy(s):
+        total = pair_sum[s, mx, gy]
+        for k, copy in enumerate(xy_copies(s)):
+            copy.wait_recv()
+            total = total + from_xy[s, k]
+        line_sum[s] = total
 
     def step(s, _):
         pair = lax.rem(gz + 1 + s, far)
@@ -209,26 +217,26 @@
         query_rows = jnp.concatenate([s1, s1, s2, s2, s1, s3, one, one, one, m1, m2, m3, zero], axis=0)
         cross[...] = jnp.exp(dot_rows(query_rows, point_rows[...])).astype(bf16)
 
+        @pl.when(s == 0)
+        def _():
+            loads[5].wait()
+
+        proj[...] = jnp.dot(cross[...], inverse[...], preferred_element_type=f32).astype(bf16)
+
         @pl.when(s >= 1)
         def _():
             after_core(s - 1)
 
-        @pl.when(s == 0)
+        @pl.when(s >= 2)
         def _():
-            load.wait()
-
-        proj[...] = jnp.dot(cross[...], inverse[...], preferred_element_type=f32).astype(bf16)
-
-        @pl.when(s >= 1)
-        def _():
-            after_x(s - 1)
+            after_xy(s - 2)
+            z_copy(s - 2).start()
 
         info = dot_lanes(values, proj[...])
         for b in range(2):
             rows = slice(b * batch, (b + 1) * batch)
-            left = jnp.concatenate([proj[rows, :], cross[rows, :]], axis=1)
-            right = jnp.concatenate([cross[rows, :], proj[rows, :]], axis=1)
-            term = 0.5 * dot_lanes(left, right)
+            left, right = proj[rows, :], cross[rows, :]
+            term = 0.5 * (dot_lanes(left, right) + dot_lanes(right, left))
             first, second = term[:half, :half], term[half:, half:]
             main = jnp.concatenate([jnp.where(row >= col, first, second), term[half:, :half]], axis=0)
             diagonal = jnp.sum(jnp.where(row == col, second, 0.0), axis=0, keepdims=True)
@@ -239,11 +247,6 @@
                 packed[s, e % 2, e // 2, b, share : share + 8, :] = more if e == 0 else jnp.zeros_like(more)
         core_copy(s).start()
 
-        @pl.when(s >= 1)
-        def _():
-            after_y(s - 1)
-            z_copy(s - 1).start()
-
         return 0
 
     lax.fori_loop(0, far, step, 0)
@@ -251,8 +254,9 @@
     after_core(last)
     mine = order_ref[:, pl.ds(pl.multiple_of(g * batch, batch), batch)]
     sorted_ref[...] = select(groups, members, table[...], mine, per, 1)
-    after_x(last)
-    after_y(last)
+    after_xy(last - 1)
+    z_copy(last - 1).start()
+    after_xy(last)
     total = line_sum[last]
     for s in range(last):
         z_copy(s).wait_recv()
@@ -268,9 +272,8 @@
         copy.wait_send()
     for s in range(far):
         core_copy(s).wait_send()
-        for k in range(1, near):
-            x_copy(s, k).wait_send()
-        y_copy(s).wait_send()
+        for copy in xy_copies(s):
+            copy.wait_send()
         if s < last:
             z_copy(s).wait_send()
     for copy in pieces_out:
@@ -363,9 +366,14 @@
             jax.ShapeDtypeStruct((members, size, half), f32),
             jax.ShapeDtypeStruct((1, batch), f32),
         ),
-        in_specs=in_vmem(4) + [pl.BlockSpec(memory_space=pl.ANY)] + in_vmem(1),
+        in_specs=[pl.BlockSpec(memory_space=pltpu.HBM)] * 6,
         out_specs=tuple(in_vmem(2)),
         scratch_shapes=[
+            vmem(queries.shape, f32),
+            vmem((1, queries.shape[1]), f32),
+            vmem((1, batch_order.shape[0]), jnp.int32),
+            vmem((dim, count), f32),
+            vmem((1, count), bf16),
             vmem((dim, 2 * queries.shape[1]), f32),
             vmem((members, groups, dim, 2 * queries.shape[1]), f32),
             vmem((members * groups * dim, 6 * queries.shape[1]), bf16),
@@ -376,24 +384,20 @@
             vmem((far, 2, near, 2, size, half), f32),
             vmem((far, near, 2, size, half), f32),
             vmem((far, near, 2, size, half), f32),
-            vmem((far, near - 1, 2, size, half), f32),
-            vmem((far, 2, size, half), f32),
-            vmem((far, size, half), f32),
+            vmem((far, 2 * near - 1, size, half), f32),
             vmem((far, size, half), f32),
             vmem((far - 1, size, half), f32),
             vmem((size, half), f32),
             vmem((members, size, half), f32),
-            dma,
+            dma((6,)),
             dma((groups - 1,)),
             dma((groups - 1,)),
             dma((members - 1,)),
             dma((members - 1,)),
             dma((far,)),
             dma((far,)),
-            dma((far, near - 1)),
-            dma((far, near - 1)),
-            dma((far,)),
-            dma((far,)),
+            dma((far, 2 * near - 1)),
+            dma((far, 2 * near - 1)),
             dma((far - 1,)),
             dma((far - 1,)),
             dma((members - 1,)),
@@ -401,11 +405,11 @@
         ],
         compiler_params=pltpu.CompilerParams(vmem_limit_bytes=VMEM_LIMIT, collective_id=0, has_side_effects=True),
         name="terms",
-    )(queries, prior_precision[None, :], batch_order[None, :], points[0], inverse_cov[0], targets)
+    )(queries, prior_precision[None, :], batch_order[None, :], points, inverse_cov, targets)
     return pl.pallas_call(
         functools.partial(factor_kernel, experts),
         out_shape=jax.ShapeDtypeStruct(noise.shape, f32),
-        in_specs=in_vmem(2) + [pl.BlockSpec(memory_space=pl.ANY)],
+        in_specs=in_vmem(2) + [pl.BlockSpec(memory_space=pltpu.HBM)],
         out_specs=pl.BlockSpec(memory_space=vmem),
         scratch_shapes=[
             vmem(noise.shape, f32),

time: 61.3 us -> 45.7 us (0.75)
  Pallas kernels: 55.9 us -> 45.6 us
  local copies, waits for them, and re-layouts: 5.08 us -> 0 us
    pallas_call x1, Pallas kernels: 47.1 us -> 35.1 us  [per_device(): pl.pallas_call(functools.partial(terms_kernel, groups, members, batch), o...]
    unnamed x14 -> x0, local copies, waits for them, and re-layouts: 5.08 us -> none
    pallas_call x1, Pallas kernels: 8.83 us -> 10.4 us  [per_device(): pl.pallas_call(functools.partial(factor_kernel, experts), out_shape=jax.S...]
where the time goes in v1:
time: 45.7 us; the launch traced here: 45.6 us
  Pallas kernels  45.6 us (100%)
    pallas_call x1, Pallas kernels, per_device(): pl.pallas_call(functools.partial(terms_kernel, groups, members, batch), o...  35.1 us
    pallas_call x1, Pallas kernels, per_device(): pl.pallas_call(functools.partial(factor_kernel, experts), out_shape=jax.S...  10.4 us

profile of v1, /device:TPU:0, one launch (start us, length us, event | category | flops | bytes accessed | tf_op | source)
XLA Modules:
  0.0 45.6 jit_solution(14246567626794077272)
XLA Ops:
  0.0 35.1 %terms.1 = (f32[4,72,128]{2,1,0:T(8,128)}, f32[1,256]{1,0:T(1,128)}) custom-call(f32[8,64]{1,0:T(8,128)} %queries_hbm.1, f32[1,64]{1,0:T(1,128)} %bitcast.3, s32[1,2048]{1,0:T(1,128)} %bitcast.2, f32[1,8,1024]{2,1,0:T(8,128)} %points_hbm.1, bf16[1,1024,1024]{2,1,0:T(8,128)(2,1)} %inverse_hbm.1, bf16[1,1024]{1,0:T(2,128)(2,1)} %targets_hbm.1), custom_call_target="tpu_custom_call" | custom-call | tf_op jit(solution)/shard_map/terms/pallas_call | solution.py:363
  35.2 10.4 %factor.1 = f32[256,256]{1,0:T(8,128)} custom-call(f32[4,72,128]{2,1,0:T(8,128)} %get-tuple-element.7.packed_ref, f32[1,256]{1,0:T(1,128)} %get-tuple-element.8.prior_ref, f32[256,256]{1,0:T(8,128)} %noise_hbm.1), custom_call_target="tpu_custom_call" | custom-call | tf_op jit(solution)/shard_map/factor/pallas_call | solution.py:409

commit v2 on v1

v2 whole, which is shorter than its diff:
```python
import functools

import jax
import jax.numpy as jnp
from jax import lax
from jax.experimental import pallas as pl
from jax.experimental.pallas import tpu as pltpu
from jax.sharding import PartitionSpec as P

kernel_rate = 0.25
f32, bf16 = jnp.float32, jnp.bfloat16
LEAF = 16
MESH = pl.DeviceIdType.MESH
VMEM_LIMIT = 63 * 1024 * 1024


def split3(x):
    high = x.astype(bf16)
    rest = x - high.astype(f32)
    mid = rest.astype(bf16)
    low = (rest - mid.astype(f32)).astype(bf16)
    return high, mid, low


def iota(shape, dim):
    return lax.broadcasted_iota(jnp.int32, shape, dim)


def dot_rows(a, b):
    return lax.dot_general(a, b, (((0,), (0,)), ((), ())), preferred_element_type=f32)


def dot_lanes(a, b):
    return lax.dot_general(a, b, (((1,), (1,)), ((), ())), preferred_element_type=f32)


def select(groups, members, wide, order, shift, rows):
    share = wide.shape[1] // 3
    per = share // 2
    owner = lax.shift_right_logical(order, per.bit_length() - 1)
    place = (order & (per - 1)) + shift
    onehot = jnp.where(iota((share, order.shape[1]), 0) == place, 1.0, 0.0).astype(bf16)
    found = jnp.dot(wide, jnp.concatenate([onehot] * 3, axis=0), preferred_element_type=f32)
    total = jnp.zeros((rows, order.shape[1]), f32)
    for m in range(members):
        for g in range(groups):
            at = (m * groups + g) * 8
            total = total + jnp.where(owner == g * members + m, found[at : at + rows], 0.0)
    return total


def draw_samples(experts, packed_ref, prior, noise, out_ref, work, inverse, forward):
    batch = noise.shape[0]
    half = batch // 2
    members, share = packed_ref.shape[0], packed_ref.shape[1] - 8
    main = jnp.concatenate([packed_ref[e, 0:share, :] for e in range(members)], axis=0)
    scale = 1.0 / experts
    row, col = iota((half, half), 0), iota((half, half), 1)
    mixed = main[:half] * scale
    lower = jnp.where(row >= col, mixed, 0.0)
    upper = jnp.where(row < col, mixed, 0.0)
    below = main[half:] * scale
    tail = packed_ref[0, share : share + 8, :] * scale
    first = lower + jnp.where(row < col, lower.T, 0.0)
    first = first + jnp.where(row == col, prior[:, :half], 0.0)
    second = upper + upper.T + jnp.where(row == col, tail[0:1] + prior[:, half:], 0.0)
    work[0:half, 0:half] = first
    work[0:half, half:batch] = below.T
    work[half:batch, 0:half] = below
    work[half:batch, half:batch] = second
    work[0:half, batch:] = jnp.broadcast_to(tail[1:2], (half, half)).T
    work[half:batch, batch:] = jnp.broadcast_to(tail[2:3], (half, half)).T

    width = batch + half
    sub = iota((LEAF, half), 0)
    wide_sub, lane = iota((LEAF, width), 0), iota((LEAF, width), 1)
    for start in range(0, batch, LEAF):
        stop = start + LEAF
        rows = work[start:stop, :]
        cols = [jnp.broadcast_to(rows[:, start + k : start + k + 1], (LEAF, half)) for k in range(LEAF)]
        rows = jnp.where((lane >= start) & (lane < stop), jnp.where(lane - start == wide_sub, 1.0, 0.0), rows)
        pivots = jnp.ones((LEAF, half), f32)
        for j in range(LEAF):
            pivot = jnp.broadcast_to(cols[j][j : j + 1], (LEAF, half))
            pivots = jnp.where(sub == j, pivot, pivots)
            if j + 1 < LEAF:
                factor = jnp.where(sub > j, cols[j] * (1.0 / pivot), 0.0)
                for k in range(j + 1, LEAF):
                    cols[k] = cols[k] - factor * cols[k][j : j + 1]
                rows = rows - jnp.concatenate([factor] * 3, axis=1) * rows[j : j + 1]
        rows = rows * jnp.concatenate([lax.rsqrt(pivots)] * 3, axis=1)
        inverse[start:stop, :] = jnp.where(lane < stop, rows, 0.0)[:, :batch]
        forward[start:stop, :] = rows[:, batch:]
        if stop < batch:
            base = stop // half * half
            a1, a2, a3 = split3(rows)
            right = jnp.concatenate([a1, a2, a1, a2, a3, a1], axis=0)
            left = jnp.concatenate([a1, a1, a2, a2, a1, a3], axis=0)[:, base:batch]
            update = dot_rows(left, right)[stop - base :]
            rest = work[stop:batch, :]
            inside = iota(rest.shape, 1)
            rest = jnp.where((inside >= start) & (inside < stop), 0.0, rest)
            work[stop:batch, :] = rest - update

    side = noise[...] + jnp.concatenate([forward[...]] * 2, axis=1)
    out_ref[...] = lax.dot_general(
        inverse[...], side, (((0,), (0,)), ((), ())), precision=lax.Precision.HIGHEST, preferred_element_type=f32
    )


def samples_kernel(
    groups,
    members,
    batch,
    experts,
    queries_hbm,
    prior_hbm,
    order_hbm,
    points_hbm,
    inverse_hbm,
    targets_hbm,
    noise_hbm,
    out_ref,
    queries_ref,
    prior_ref,
    order_ref,
    points_ref,
    targets_ref,
    own,
    gathered,
    table,
    inverse,
    point_rows,
    cross,
    proj,
    packed,
    from_core,
    pair_sum,
    from_xy,
    line_sum,
    from_z,
    piece,
    whole,
    noise,
    work,
    factored,
    forward,
    load_sems,
    row_send,
    row_recv,
    block_send,
    block_recv,
    core_send,
    core_recv,
    xy_send,
    xy_recv,
    z_send,
    z_recv,
    last_send,
    last_recv,
):
    g, m = lax.axis_index("group"), lax.axis_index("member")
    far, near = groups // 2, members // 2
    gz, gy = g // 2, g % 2
    mx, mc = m // 2, m % 2
    half = batch // 2
    chunk = 2 * batch
    share = batch // members

    sources = (queries_hbm, prior_hbm, points_hbm.at[0], order_hbm, targets_hbm, inverse_hbm.at[0], noise_hbm)
    places = (queries_ref, prior_ref, points_ref, order_ref, targets_ref, inverse, noise)
    loads = [pltpu.make_async_copy(a, b, load_sems.at[i]) for i, (a, b) in enumerate(zip(sources, places))]
    for load in loads:
        load.start()

    def other_group(k):
        return lax.rem(g + k, groups), m

    def other_member(k):
        return g, lax.rem(m + k, members)

    def line_peer(k):
        return lax.rem(gz + k, far) * 2 + gy, m

    core_peer = (g, m + 1 - 2 * mc)

    barrier = pltpu.get_barrier_semaphore()
    for k in range(1, groups):
        pl.semaphore_signal(barrier, inc=1, device_id=other_group(k), device_id_type=MESH)
    for k in range(1, members):
        pl.semaphore_signal(barrier, inc=1, device_id=other_member(k), device_id_type=MESH)

    per = queries_ref.shape[1]
    for load in loads[:2]:
        load.wait()
    own[...] = jnp.concatenate(
        [queries_ref[...], jnp.broadcast_to(prior_ref[...], (8, per))], axis=1
    )
    pl.semaphore_wait(barrier, groups + members - 2)

    def remote(src, dst, send, recv, device):
        return pltpu.make_async_remote_copy(
            src_ref=src, dst_ref=dst, send_sem=send, recv_sem=recv, device_id=device, device_id_type=MESH
        )

    rows_out = [
        remote(own, gathered.at[m, g], row_send.at[k - 1], row_recv.at[k - 1], other_group(k)) for k in range(1, groups)
    ]
    for copy in rows_out:
        copy.start()
    gathered[m, g] = own[...]

    for load in loads[2:5]:
        load.wait()
    coords = points_ref[...]
    count = coords.shape[1]
    p1, p2, p3 = split3(coords)
    n1, n2, n3 = split3(-kernel_rate * jnp.sum(coords * coords, axis=0, keepdims=True))
    ones = jnp.ones((1, count), bf16)
    none = jnp.zeros((10, count), bf16)
    point_rows[...] = jnp.concatenate([p1, p2, p1, p2, p3, p1, n1, n2, n3, ones, ones, ones, none], axis=0)
    row, col = iota((half, half), 0), iota((half, half), 1)
    values = jnp.broadcast_to(targets_ref[...].astype(f32), (16, count)).astype(bf16)

    for copy in rows_out:
        copy.wait_recv()
    blocks_out = [
        remote(gathered.at[m], gathered.at[m], block_send.at[k - 1], block_recv.at[k - 1], other_member(k))
        for k in range(1, members)
    ]
    for copy in blocks_out:
        copy.start()
    for copy in blocks_out:
        copy.wait_recv()
    for e in range(members):
        tiles = gathered[e].reshape(groups * 8, own.shape[1])
        table[e * groups * 8 : (e + 1) * groups * 8, :] = jnp.concatenate(split3(tiles), axis=1)

    def core_copy(s):
        return remote(packed.at[s, 1 - mc], from_core.at[s], core_send.at[s], core_recv.at[s], core_peer)

    def xy_copies(s):
        copies = []
        for k in range(1, 2 * near):
            peer, to = lax.rem(mx + k // 2, near), lax.rem(gy + k % 2, 2)
            copies.append(
                remote(
                    pair_sum.at[s, peer, to],
                    from_xy.at[s, k - 1],
                    xy_send.at[s, k - 1],
                    xy_recv.at[s, k - 1],
                    (gz * 2 + to, peer * 2 + mc),
                )
            )
        return copies

    def z_copy(s):
        return remote(line_sum.at[s], from_z.at[s], z_send.at[s], z_recv.at[s], line_peer(s + 1))

    def after_core(s):
        core_copy(s).wait_recv()
        pair_sum[s] = packed[s, mc] + from_core[s]
        for copy in xy_copies(s):
            copy.start()

    def after_xy(s):
        total = pair_sum[s, mx, gy]
        for k, copy in enumerate(xy_copies(s)):
            copy.wait_recv()
            total = total + from_xy[s, k]
        line_sum[s] = total

    def step(s, _):
        pair = lax.rem(gz + 1 + s, far)
        order = order_ref[:, pl.ds(pl.multiple_of(pair * chunk, chunk), chunk)]
        q = select(groups, members, table[...], order, 0, 8)
        m1, m2, m3 = split3(-kernel_rate * jnp.sum(q * q, axis=0, keepdims=True))
        s1, s2, s3 = split3(2.0 * kernel_rate * q)
        one = jnp.ones((1, chunk), bf16)
        zero = jnp.zeros((10, chunk), bf16)
        query_rows = jnp.concatenate([s1, s1, s2, s2, s1, s3, one, one, one, m1, m2, m3, zero], axis=0)
        cross[...] = jnp.exp(dot_rows(query_rows, point_rows[...])).astype(bf16)

        proj[...] = jnp.dot(cross[...], inverse[...], preferred_element_type=f32).astype(bf16)

        for b in range(2):
            rows = slice(b * batch, (b + 1) * batch)
            left, right = proj[rows, :], cross[rows, :]
            product = dot_lanes(jnp.concatenate([right, values], axis=0), left)
            term = 0.5 * (dot_lanes(left, right) + product[:batch])
            first, second = term[:half, :half], term[half:, half:]
            main = jnp.concatenate([jnp.where(row >= col, first, second), term[half:, :half]], axis=0)
            diagonal = jnp.sum(jnp.where(row == col, second, 0.0), axis=0, keepdims=True)
            line = product[batch : batch + 1]
            more = jnp.concatenate([diagonal, line[:, :half], line[:, half:], jnp.zeros((5, half), f32)], axis=0)
            for e in range(members):
                packed[s, e % 2, e // 2, b, 0:share, :] = main[e * share : (e + 1) * share]
                packed[s, e % 2, e // 2, b, share : share + 8, :] = more if e == 0 else jnp.zeros_like(more)
        core_copy(s).start()

        @pl.when(s >= 1)
        def _():
            after_core(s - 1)

        @pl.when(s >= 2)
        def _():
            after_xy(s - 2)
            z_copy(s - 2).start()

        return 0

    loads[5].wait()
    lax.fori_loop(0, far, step, 0)
    last = far - 1
    after_core(last)
    mine = order_ref[:, pl.ds(pl.multiple_of(g * batch, batch), batch)]
    prior = select(groups, members, table[...], mine, per, 1)
    after_xy(last - 1)
    z_copy(last - 1).start()
    after_xy(last)
    total = line_sum[last]
    for s in range(last):
        z_copy(s).wait_recv()
        total = total + from_z[s]
    piece[...] = total
    pieces_out = [
        remote(piece, whole.at[m], last_send.at[k - 1], last_recv.at[k - 1], other_member(k)) for k in range(1, members)
    ]
    for copy in pieces_out:
        copy.start()
    whole[m] = total
    for copy in pieces_out:
        copy.wait_recv()
    loads[6].wait()
    draw_samples(experts, whole, prior, noise, out_ref, work, factored, forward)
    for copy in rows_out + blocks_out:
        copy.wait_send()
    for s in range(far):
        core_copy(s).wait_send()
        for copy in xy_copies(s):
            copy.wait_send()
        if s < last:
            z_copy(s).wait_send()
    for copy in pieces_out:
        copy.wait_send()


def per_device(points, inverse_cov, targets, queries, prior_precision, batch_order, noise):
    batch = noise.shape[0]
    groups = lax.axis_size("group")
    members = lax.axis_size("member")
    experts = points.shape[0] * groups * members
    half = batch // 2
    far, near = groups // 2, members // 2
    size = batch // members + 8
    dim, count = points.shape[1:]
    vmem, dma = pltpu.VMEM, pltpu.SemaphoreType.DMA
    return pl.pallas_call(
        functools.partial(samples_kernel, groups, members, batch, experts),
        out_shape=jax.ShapeDtypeStruct(noise.shape, f32),
        in_specs=[pl.BlockSpec(memory_space=pltpu.HBM)] * 7,
        out_specs=pl.BlockSpec(memory_space=vmem),
        scratch_shapes=[
            vmem(queries.shape, f32),
            vmem((1, queries.shape[1]), f32),
            vmem((1, batch_order.shape[0]), jnp.int32),
            vmem((dim, count), f32),
            vmem((1, count), bf16),
            vmem((dim, 2 * queries.shape[1]), f32),
            vmem((members, groups, dim, 2 * queries.shape[1]), f32),
            vmem((members * groups * dim, 6 * queries.shape[1]), bf16),
            vmem((count, count), bf16),
            vmem((64, count), bf16),
            vmem((2 * batch, count), bf16),
            vmem((2 * batch, count), bf16),
            vmem((far, 2, near, 2, size, half), f32),
            vmem((far, near, 2, size, half), f32),
            vmem((far, near, 2, size, half), f32),
            vmem((far, 2 * near - 1, size, half), f32),
            vmem((far, size, half), f32),
            vmem((far - 1, size, half), f32),
            vmem((size, half), f32),
            vmem((members, size, half), f32),
            vmem(noise.shape, f32),
            vmem((batch, batch + half), f32),
            vmem((batch, batch), f32),
            vmem((batch, half), f32),
            dma((7,)),
            dma((groups - 1,)),
            dma((groups - 1,)),
            dma((members - 1,)),
            dma((members - 1,)),
            dma((far,)),
            dma((far,)),
            dma((far, 2 * near - 1)),
            dma((far, 2 * near - 1)),
            dma((far - 1,)),
            dma((far - 1,)),
            dma((members - 1,)),
            dma((members - 1,)),
        ],
        compiler_params=pltpu.CompilerParams(vmem_limit_bytes=VMEM_LIMIT, collective_id=0, has_side_effects=True),
        name="samples",
    )(queries, prior_precision[None, :], batch_order[None, :], points, inverse_cov, targets, noise)


def solution(mesh):
    return jax.shard_map(
        per_device,
        mesh=mesh,
        in_specs=(
            P(("group", "member"), None, None),
            P(("group", "member"), None, None),
            P(("group", "member"), None),
            P(None, ("group", "member")),
            P(("group", "member")),
            P(),
            P("group", "member"),
        ),
        out_specs=P("group", "member"),
        check_vma=False,
    )
```

time: 45.7 us -> 44.3 us (0.969)
  Pallas kernels: 45.6 us -> 42.5 us
  local copies, waits for them, and re-layouts: 0 us -> 1.67 us
    pallas_call x2 -> x1, Pallas kernels: 45.6 us -> 42.5 us  [per_device(): pl.pallas_call(functools.partial(samples_kernel, groups, members, batch,...]
    unnamed x0 -> x1, local copies, waits for them, and re-layouts: none -> 1.67 us
where the time goes in v2:
time: 44.3 us; the launch traced here: 44.1 us
  Pallas kernels  42.5 us (96%)
  local copies, waits for them, and re-layouts  1.67 us (4%)
    pallas_call x1, Pallas kernels, per_device(): pl.pallas_call(functools.partial(samples_kernel, groups, members, batch,...  42.5 us
    unnamed x1, local copies, waits for them, and re-layouts  1.67 us

profile of v2, /device:TPU:0, one launch (start us, length us, event | category | flops | bytes accessed | tf_op | source)
XLA Modules:
  0.0 44.1 jit_solution(1946797303667900213)
XLA Ops:
  0.0 42.5 %samples.1 = f32[256,256]{1,0:T(8,128)} custom-call(f32[8,64]{1,0:T(8,128)} %queries_hbm.1, f32[1,64]{1,0:T(1,128)} %bitcast.3, s32[1,2048]{1,0:T(1,128)} %bitcast.2, f32[1,8,1024]{2,1,0:T(8,128)} %points_hbm.1, bf16[1,1024,1024]{2,1,0:T(8,128)(2,1)} %inverse_hbm.1, bf16[1,1024]{1,0:T(2,128)(2,1)} %targets_hbm.1, f32[256,256]{1,0:T(8,128)} %noise_hbm.1), custom_call_target="tpu_custom_call" | custom-call | tf_op jit(solution)/shard_map/samples/pallas_call | solution.py:358
  42.5 1.7 %copy.9 = f32[256,256]{1,0:T(8,128)} copy(f32[256,256]{1,0:T(8,128)} %samples.1) | data formatting | bytes 524288

commit v3 on v2

--- a/solution.py
+++ b/solution.py
@@ -80,14 +80,25 @@
         cols = [jnp.broadcast_to(rows[:, start + k : start + k + 1], (LEAF, half)) for k in range(LEAF)]
         rows = jnp.where((lane >= start) & (lane < stop), jnp.where(lane - start == wide_sub, 1.0, 0.0), rows)
         pivots = jnp.ones((LEAF, half), f32)
-        for j in range(LEAF):
-            pivot = jnp.broadcast_to(cols[j][j : j + 1], (LEAF, half))
-            pivots = jnp.where(sub == j, pivot, pivots)
-            if j + 1 < LEAF:
-                factor = jnp.where(sub > j, cols[j] * (1.0 / pivot), 0.0)
-                for k in range(j + 1, LEAF):
-                    cols[k] = cols[k] - factor * cols[k][j : j + 1]
-                rows = rows - jnp.concatenate([factor] * 3, axis=1) * rows[j : j + 1]
+        for j in range(0, LEAF, 2):
+            after, other = cols[j], cols[j + 1]
+            a = jnp.broadcast_to(after[j : j + 1], (LEAF, half))
+            b = jnp.broadcast_to(after[j + 1 : j + 2], (LEAF, half))
+            c = jnp.broadcast_to(other[j + 1 : j + 2], (LEAF, half))
+            det = a * c - b * b
+            over_a, over_det = pl.reciprocal(a, approx=True), pl.reciprocal(det, approx=True)
+            slope = b * over_a
+            pivots = jnp.where(sub == j, a, jnp.where(sub == j + 1, det * over_a, pivots))
+            second = jnp.where(sub > j + 1, (other - after * slope) * (a * over_det), 0.0)
+            first = jnp.where(sub > j + 1, (after - b * second) * over_a, 0.0)
+            for k in range(j + 2, LEAF):
+                cols[k] = cols[k] - first * cols[k][j : j + 1] - second * cols[k][j + 1 : j + 2]
+            first = jnp.where(sub == j + 1, slope, first)
+            rows = (
+                rows
+                - jnp.concatenate([first] * 3, axis=1) * rows[j : j + 1]
+                - jnp.concatenate([second] * 3, axis=1) * rows[j + 1 : j + 2]
+            )
         rows = rows * jnp.concatenate([lax.rsqrt(pivots)] * 3, axis=1)
         inverse[start:stop, :] = jnp.where(lane < stop, rows, 0.0)[:, :batch]
         forward[start:stop, :] = rows[:, batch:]
@@ -139,6 +150,7 @@
     from_xy,
     line_sum,
     from_z,
+    from_own,
     piece,
     whole,
     noise,
@@ -156,6 +168,8 @@
     xy_recv,
     z_send,
     z_recv,
+    own_send,
+    own_recv,
     last_send,
     last_recv,
 ):
@@ -270,6 +284,8 @@
             total = total + from_xy[s, k]
         line_sum[s] = total
 
+    last = far - 1
+
     def step(s, _):
         pair = lax.rem(gz + 1 + s, far)
         order = order_ref[:, pl.ds(pl.multiple_of(pair * chunk, chunk), chunk)]
@@ -282,6 +298,16 @@
         cross[...] = jnp.exp(dot_rows(query_rows, point_rows[...])).astype(bf16)
 
         proj[...] = jnp.dot(cross[...], inverse[...], preferred_element_type=f32).astype(bf16)
+
+
+        @pl.when(s >= 1)
+        def _():
+            after_core(s - 1)
+
+        @pl.when(s >= 2)
+        def _():
+            after_xy(s - 2)
+            z_copy(s - 2).start()
 
         for b in range(2):
             rows = slice(b * batch, (b + 1) * batch)
@@ -296,29 +322,37 @@
             for e in range(members):
                 packed[s, e % 2, e // 2, b, 0:share, :] = main[e * share : (e + 1) * share]
                 packed[s, e % 2, e // 2, b, share : share + 8, :] = more if e == 0 else jnp.zeros_like(more)
-        core_copy(s).start()
-
-        @pl.when(s >= 1)
+
+        @pl.when(s < last)
         def _():
-            after_core(s - 1)
-
-        @pl.when(s >= 2)
-        def _():
-            after_xy(s - 2)
-            z_copy(s - 2).start()
+            core_copy(s).start()
 
         return 0
 
     loads[5].wait()
     lax.fori_loop(0, far, step, 0)
-    last = far - 1
-    after_core(last)
+    own_out = []
+    for k in range(1, 2 * members):
+        to, peer = lax.rem(gy + k % 2, 2), lax.rem(m + k // 2, members)
+        own_out.append(
+            remote(
+                packed.at[last, peer % 2, peer // 2, to],
+                from_own.at[k - 1],
+                own_send.at[k - 1],
+                own_recv.at[k - 1],
+                (gz * 2 + to, peer),
+            )
+        )
+    for copy in own_out:
+        copy.start()
     mine = order_ref[:, pl.ds(pl.multiple_of(g * batch, batch), batch)]
     prior = select(groups, members, table[...], mine, per, 1)
     after_xy(last - 1)
     z_copy(last - 1).start()
-    after_xy(last)
-    total = line_sum[last]
+    total = packed[last, mc, mx, gy]
+    for k, copy in enumerate(own_out):
+        copy.wait_recv()
+        total = total + from_own[k]
     for s in range(last):
         z_copy(s).wait_recv()
         total = total + from_z[s]
@@ -335,12 +369,13 @@
     draw_samples(experts, whole, prior, noise, out_ref, work, factored, forward)
     for copy in rows_out + blocks_out:
         copy.wait_send()
-    for s in range(far):
+    for copy in own_out:
+        copy.wait_send()
+    for s in range(last):
         core_copy(s).wait_send()
         for copy in xy_copies(s):
             copy.wait_send()
-        if s < last:
-            z_copy(s).wait_send()
+        z_copy(s).wait_send()
     for copy in pieces_out:
         copy.wait_send()
 
@@ -374,11 +409,12 @@
             vmem((2 * batch, count), bf16),
             vmem((2 * batch, count), bf16),
             vmem((far, 2, near, 2, size, half), f32),
-            vmem((far, near, 2, size, half), f32),
-            vmem((far, near, 2, size, half), f32),
-            vmem((far, 2 * near - 1, size, half), f32),
-            vmem((far, size, half), f32),
+            vmem((far - 1, near, 2, size, half), f32),
+            vmem((far - 1, near, 2, size, half), f32),
+            vmem((far - 1, 2 * near - 1, size, half), f32),
             vmem((far - 1, size, half), f32),
+            vmem((far - 1, size, half), f32),
+            vmem((2 * members - 1, size, half), f32),
             vmem((size, half), f32),
             vmem((members, size, half), f32),
             vmem(noise.shape, f32),
@@ -390,12 +426,14 @@
             dma((groups - 1,)),
             dma((members - 1,)),
             dma((members - 1,)),
-            dma((far,)),
-            dma((far,)),
-            dma((far, 2 * near - 1)),
-            dma((far, 2 * near - 1)),
             dma((far - 1,)),
             dma((far - 1,)),
+            dma((far - 1, 2 * near - 1)),
+            dma((far - 1, 2 * near - 1)),
+            dma((far - 1,)),
+            dma((far - 1,)),
+            dma((2 * members - 1,)),
+            dma((2 * members - 1,)),
             dma((members - 1,)),
             dma((members - 1,)),
         ],

time: 44.3 us -> 44.8 us (1.011)
    pallas_call x1, Pallas kernels: 42.5 us -> 42.9 us  [per_device(): pl.pallas_call(functools.partial(samples_kernel, groups, members, batch,...]
where the time goes in v3:
time: 44.8 us; the launch traced here: 44.6 us
  Pallas kernels  42.9 us (96%)
  local copies, waits for them, and re-layouts  1.67 us (4%)
    pallas_call x1, Pallas kernels, per_device(): pl.pallas_call(functools.partial(samples_kernel, groups, members, batch,...  42.9 us
    unnamed x1, local copies, waits for them, and re-layouts  1.67 us

profile of v3, /device:TPU:0, one launch (start us, length us, event | category | flops | bytes accessed | tf_op | source)
XLA Modules:
  0.0 44.6 jit_solution(4210813612368887961)
XLA Ops:
  0.0 42.9 %samples.1 = f32[256,256]{1,0:T(8,128)} custom-call(f32[8,64]{1,0:T(8,128)} %queries_hbm.1, f32[1,64]{1,0:T(1,128)} %bitcast.3, s32[1,2048]{1,0:T(1,128)} %bitcast.2, f32[1,8,1024]{2,1,0:T(8,128)} %points_hbm.1, bf16[1,1024,1024]{2,1,0:T(8,128)(2,1)} %inverse_hbm.1, bf16[1,1024]{1,0:T(2,128)(2,1)} %targets_hbm.1, f32[256,256]{1,0:T(8,128)} %noise_hbm.1), custom_call_target="tpu_custom_call" | custom-call | tf_op jit(solution)/shard_map/samples/pallas_call | solution.py:393
  42.9 1.7 %copy.9 = f32[256,256]{1,0:T(8,128)} copy(f32[256,256]{1,0:T(8,128)} %samples.1) | data formatting | bytes 524288

commit v4 on v2

--- a/solution.py
+++ b/solution.py
@@ -80,14 +80,25 @@
         cols = [jnp.broadcast_to(rows[:, start + k : start + k + 1], (LEAF, half)) for k in range(LEAF)]
         rows = jnp.where((lane >= start) & (lane < stop), jnp.where(lane - start == wide_sub, 1.0, 0.0), rows)
         pivots = jnp.ones((LEAF, half), f32)
-        for j in range(LEAF):
-            pivot = jnp.broadcast_to(cols[j][j : j + 1], (LEAF, half))
-            pivots = jnp.where(sub == j, pivot, pivots)
-            if j + 1 < LEAF:
-                factor = jnp.where(sub > j, cols[j] * (1.0 / pivot), 0.0)
-                for k in range(j + 1, LEAF):
-                    cols[k] = cols[k] - factor * cols[k][j : j + 1]
-                rows = rows - jnp.concatenate([factor] * 3, axis=1) * rows[j : j + 1]
+        for j in range(0, LEAF, 2):
+            after, other = cols[j], cols[j + 1]
+            a = jnp.broadcast_to(after[j : j + 1], (LEAF, half))
+            b = jnp.broadcast_to(after[j + 1 : j + 2], (LEAF, half))
+            c = jnp.broadcast_to(other[j + 1 : j + 2], (LEAF, half))
+            det = a * c - b * b
+            over_a, over_det = pl.reciprocal(a, approx=True), pl.reciprocal(det, approx=True)
+            slope = b * over_a
+            pivots = jnp.where(sub == j, a, jnp.where(sub == j + 1, det * over_a, pivots))
+            second = jnp.where(sub > j + 1, (other - after * slope) * (a * over_det), 0.0)
+            first = jnp.where(sub > j + 1, (after - b * second) * over_a, 0.0)
+            for k in range(j + 2, LEAF):
+                cols[k] = cols[k] - first * cols[k][j : j + 1] - second * cols[k][j + 1 : j + 2]
+            first = jnp.where(sub == j + 1, slope, first)
+            rows = (
+                rows
+                - jnp.concatenate([first] * 3, axis=1) * rows[j : j + 1]
+                - jnp.concatenate([second] * 3, axis=1) * rows[j + 1 : j + 2]
+            )
         rows = rows * jnp.concatenate([lax.rsqrt(pivots)] * 3, axis=1)
         inverse[start:stop, :] = jnp.where(lane < stop, rows, 0.0)[:, :batch]
         forward[start:stop, :] = rows[:, batch:]
@@ -148,8 +159,8 @@
     load_sems,
     row_send,
     row_recv,
-    block_send,
-    block_recv,
+    tile_send,
+    tile_recv,
     core_send,
     core_recv,
     xy_send,
@@ -206,10 +217,19 @@
     rows_out = [
         remote(own, gathered.at[m, g], row_send.at[k - 1], row_recv.at[k - 1], other_group(k)) for k in range(1, groups)
     ]
-    for copy in rows_out:
+
+    def tile_copies(k):
+        at = lax.rem(g + groups - k, groups)
+        source = gathered.at[m, at] if k else own
+        return [
+            remote(source, gathered.at[m, at], tile_send.at[k, j - 1], tile_recv.at[k, j - 1], other_member(j))
+            for j in range(1, members)
+        ]
+
+    tiles_out = [tile_copies(k) for k in range(groups)]
+    for copy in rows_out + tiles_out[0]:
         copy.start()
     gathered[m, g] = own[...]
-
     for load in loads[2:5]:
         load.wait()
     coords = points_ref[...]
@@ -222,16 +242,13 @@
     row, col = iota((half, half), 0), iota((half, half), 1)
     values = jnp.broadcast_to(targets_ref[...].astype(f32), (16, count)).astype(bf16)
 
-    for copy in rows_out:
-        copy.wait_recv()
-    blocks_out = [
-        remote(gathered.at[m], gathered.at[m], block_send.at[k - 1], block_recv.at[k - 1], other_member(k))
-        for k in range(1, members)
-    ]
-    for copy in blocks_out:
-        copy.start()
-    for copy in blocks_out:
-        copy.wait_recv()
+    for k in range(1, groups):
+        rows_out[k - 1].wait_recv()
+        for copy in tiles_out[k]:
+            copy.start()
+    for copies in tiles_out:
+        for copy in copies:
+            copy.wait_recv()
     for e in range(members):
         tiles = gathered[e].reshape(groups * 8, own.shape[1])
         table[e * groups * 8 : (e + 1) * groups * 8, :] = jnp.concatenate(split3(tiles), axis=1)
@@ -333,8 +350,9 @@
         copy.wait_recv()
     loads[6].wait()
     draw_samples(experts, whole, prior, noise, out_ref, work, factored, forward)
-    for copy in rows_out + blocks_out:
-        copy.wait_send()
+    for copies in [rows_out] + tiles_out:
+        for copy in copies:
+            copy.wait_send()
     for s in range(far):
         core_copy(s).wait_send()
         for copy in xy_copies(s):
@@ -388,8 +406,8 @@
             dma((7,)),
             dma((groups - 1,)),
             dma((groups - 1,)),
-            dma((members - 1,)),
-            dma((members - 1,)),
+            dma((groups, members - 1)),
+            dma((groups, members - 1)),
             dma((far,)),
             dma((far,)),
             dma((far, 2 * near - 1)),

time: 44.3 us -> 44.7 us (level)
  no operation moved by 1% of the time
where the time goes in v4:
time: 44.7 us; the launch traced here: 44.5 us
  Pallas kernels  42.8 us (96%)
  local copies, waits for them, and re-layouts  1.67 us (4%)
    pallas_call x1, Pallas kernels, per_device(): pl.pallas_call(functools.partial(samples_kernel, groups, members, batch,...  42.8 us
    unnamed x1, local copies, waits for them, and re-layouts  1.67 us

profile of v4, /device:TPU:0, one launch (start us, length us, event | category | flops | bytes accessed | tf_op | source)
XLA Modules:
  0.0 44.5 jit_solution(452200909883418998)
XLA Ops:
  0.0 42.8 %samples.1 = f32[256,256]{1,0:T(8,128)} custom-call(f32[8,64]{1,0:T(8,128)} %queries_hbm.1, f32[1,64]{1,0:T(1,128)} %bitcast.3, s32[1,2048]{1,0:T(1,128)} %bitcast.2, f32[1,8,1024]{2,1,0:T(8,128)} %points_hbm.1, bf16[1,1024,1024]{2,1,0:T(8,128)(2,1)} %inverse_hbm.1, bf16[1,1024]{1,0:T(2,128)(2,1)} %targets_hbm.1, f32[256,256]{1,0:T(8,128)} %noise_hbm.1), custom_call_target="tpu_custom_call" | custom-call | tf_op jit(solution)/shard_map/samples/pallas_call | solution.py:376
  42.8 1.7 %copy.9 = f32[256,256]{1,0:T(8,128)} copy(f32[256,256]{1,0:T(8,128)} %samples.1) | data formatting | bytes 524288

commit v5 on v2

--- a/solution.py
+++ b/solution.py
@@ -10,6 +10,7 @@
 kernel_rate = 0.25
 f32, bf16 = jnp.float32, jnp.bfloat16
 LEAF = 16
+PARTS = 4
 MESH = pl.DeviceIdType.MESH
 VMEM_LIMIT = 63 * 1024 * 1024
 
@@ -84,7 +85,7 @@
             pivot = jnp.broadcast_to(cols[j][j : j + 1], (LEAF, half))
             pivots = jnp.where(sub == j, pivot, pivots)
             if j + 1 < LEAF:
-                factor = jnp.where(sub > j, cols[j] * (1.0 / pivot), 0.0)
+                factor = jnp.where(sub > j, cols[j] * pl.reciprocal(pivot, approx=True), 0.0)
                 for k in range(j + 1, LEAF):
                     cols[k] = cols[k] - factor * cols[k][j : j + 1]
                 rows = rows - jnp.concatenate([factor] * 3, axis=1) * rows[j : j + 1]
@@ -283,6 +284,10 @@
 
         proj[...] = jnp.dot(cross[...], inverse[...], preferred_element_type=f32).astype(bf16)
 
+        @pl.when(s >= 1)
+        def _():
+            after_core(s - 1)
+
         for b in range(2):
             rows = slice(b * batch, (b + 1) * batch)
             left, right = proj[rows, :], cross[rows, :]
@@ -297,10 +302,6 @@
                 packed[s, e % 2, e // 2, b, 0:share, :] = main[e * share : (e + 1) * share]
                 packed[s, e % 2, e // 2, b, share : share + 8, :] = more if e == 0 else jnp.zeros_like(more)
         core_copy(s).start()
-
-        @pl.when(s >= 1)
-        def _():
-            after_core(s - 1)
 
         @pl.when(s >= 2)
         def _():
@@ -345,6 +346,18 @@
         copy.wait_send()
 
 
+def hand_over_kernel(from_ref, to_ref, sems):
+    rows = from_ref.shape[0] // PARTS
+    copies = []
+    for i in range(PARTS):
+        at = pl.ds(i * rows, rows)
+        copies.append(pltpu.make_async_copy(from_ref.at[at, :], to_ref.at[at, :], sems.at[i]))
+    for copy in copies:
+        copy.start()
+    for copy in copies:
+        copy.wait()
+
+
 def per_device(points, inverse_cov, targets, queries, prior_precision, batch_order, noise):
     batch = noise.shape[0]
     groups = lax.axis_size("group")
@@ -355,7 +368,7 @@
     size = batch // members + 8
     dim, count = points.shape[1:]
     vmem, dma = pltpu.VMEM, pltpu.SemaphoreType.DMA
-    return pl.pallas_call(
+    samples = pl.pallas_call(
         functools.partial(samples_kernel, groups, members, batch, experts),
         out_shape=jax.ShapeDtypeStruct(noise.shape, f32),
         in_specs=[pl.BlockSpec(memory_space=pltpu.HBM)] * 7,
@@ -402,6 +415,15 @@
         compiler_params=pltpu.CompilerParams(vmem_limit_bytes=VMEM_LIMIT, collective_id=0, has_side_effects=True),
         name="samples",
     )(queries, prior_precision[None, :], batch_order[None, :], points, inverse_cov, targets, noise)
+    return pl.pallas_call(
+        hand_over_kernel,
+        out_shape=jax.ShapeDtypeStruct(noise.shape, f32),
+        in_specs=[pl.BlockSpec(memory_space=pltpu.HBM)],
+        out_specs=pl.BlockSpec(memory_space=pltpu.HBM),
+        scratch_shapes=[dma((PARTS,))],
+        compiler_params=pltpu.CompilerParams(vmem_limit_bytes=VMEM_LIMIT),
+        name="hand_over",
+    )(samples)
 
 
 def solution(mesh):

time: 44.3 us -> 51.2 us (1.16)
  Pallas kernels: 42.5 us -> 51 us
  local copies, waits for them, and re-layouts: 1.67 us -> 0 us
    pallas_call x0 -> x1, Pallas kernels: none -> 9.08 us  [per_device(): pl.pallas_call(hand_over_kernel, out_shape=jax.ShapeDtypeStruct(noise.sha...]
    unnamed x1 -> x0, local copies, waits for them, and re-layouts: 1.67 us -> none
    pallas_call x1, Pallas kernels: 42.5 us -> 41.9 us  [per_device(): pl.pallas_call(functools.partial(samples_kernel, groups, members, batch,...]
where the time goes in v5:
time: 51.2 us; the launch traced here: 51 us
  Pallas kernels  51 us (100%)
    pallas_call x1, Pallas kernels, per_device(): pl.pallas_call(functools.partial(samples_kernel, groups, members, batch,...  41.9 us
    pallas_call x1, Pallas kernels, per_device(): pl.pallas_call(hand_over_kernel, out_shape=jax.ShapeDtypeStruct(noise.sha...  9.08 us

profile of v5, /device:TPU:0, one launch (start us, length us, event | category | flops | bytes accessed | tf_op | source)
XLA Modules:
  0.0 51.0 jit_solution(3938288549135124803)
XLA Ops:
  0.0 41.9 %samples.1.from_ref = f32[256,256]{1,0:T(8,128)} custom-call(f32[8,64]{1,0:T(8,128)} %queries_hbm.1, f32[1,64]{1,0:T(1,128)} %bitcast.3, s32[1,2048]{1,0:T(1,128)} %bitcast.2, f32[1,8,1024]{2,1,0:T(8,128)} %points_hbm.1, bf16[1,1024,1024]{2,1,0:T(8,128)(2,1)} %inverse_hbm.1, bf16[1,1024]{1,0:T(2,128)(2,1)} %targets_hbm.1, f32[256,256]{1,0:T(8,128)} %noise_hbm.1), custom_call_target="tpu_custom_call" | custom-call | tf_op jit(solution)/shard_map/samples/pallas_call | solution.py:371
  41.9 9.1 %hand_over.1 = f32[256,256]{1,0:T(8,128)} custom-call(f32[256,256]{1,0:T(8,128)} %samples.1.from_ref), custom_call_target="tpu_custom_call" | custom-call | tf_op jit(solution)/shard_map/hand_over/pallas_call | solution.py:418

commit v6 on v2

--- a/solution.py
+++ b/solution.py
@@ -84,7 +84,7 @@
             pivot = jnp.broadcast_to(cols[j][j : j + 1], (LEAF, half))
             pivots = jnp.where(sub == j, pivot, pivots)
             if j + 1 < LEAF:
-                factor = jnp.where(sub > j, cols[j] * (1.0 / pivot), 0.0)
+                factor = jnp.where(sub > j, cols[j] * pl.reciprocal(pivot, approx=True), 0.0)
                 for k in range(j + 1, LEAF):
                     cols[k] = cols[k] - factor * cols[k][j : j + 1]
                 rows = rows - jnp.concatenate([factor] * 3, axis=1) * rows[j : j + 1]
@@ -283,6 +283,10 @@
 
         proj[...] = jnp.dot(cross[...], inverse[...], preferred_element_type=f32).astype(bf16)
 
+        @pl.when(s >= 1)
+        def _():
+            after_core(s - 1)
+
         for b in range(2):
             rows = slice(b * batch, (b + 1) * batch)
             left, right = proj[rows, :], cross[rows, :]
@@ -297,10 +301,6 @@
                 packed[s, e % 2, e // 2, b, 0:share, :] = main[e * share : (e + 1) * share]
                 packed[s, e % 2, e // 2, b, share : share + 8, :] = more if e == 0 else jnp.zeros_like(more)
         core_copy(s).start()
-
-        @pl.when(s >= 1)
-        def _():
-            after_core(s - 1)
 
         @pl.when(s >= 2)
         def _():

time: 44.3 us -> 43.7 us (0.986)
  Pallas kernels: 42.5 us -> 41.9 us
    pallas_call x1, Pallas kernels: 42.5 us -> 41.9 us  [per_device(): pl.pallas_call(functools.partial(samples_kernel, groups, members, batch,...]
where the time goes in v6:
time: 43.7 us; the launch traced here: 43.6 us
  Pallas kernels  41.9 us (96%)
  local copies, waits for them, and re-layouts  1.67 us (4%)
    pallas_call x1, Pallas kernels, per_device(): pl.pallas_call(functools.partial(samples_kernel, groups, members, batch,...  41.9 us
    unnamed x1, local copies, waits for them, and re-layouts  1.67 us

profile of v6, /device:TPU:0, one launch (start us, length us, event | category | flops | bytes accessed | tf_op | source)
XLA Modules:
  0.0 43.6 jit_solution(912597812534272604)
XLA Ops:
  0.0 41.9 %samples.1 = f32[256,256]{1,0:T(8,128)} custom-call(f32[8,64]{1,0:T(8,128)} %queries_hbm.1, f32[1,64]{1,0:T(1,128)} %bitcast.3, s32[1,2048]{1,0:T(1,128)} %bitcast.2, f32[1,8,1024]{2,1,0:T(8,128)} %points_hbm.1, bf16[1,1024,1024]{2,1,0:T(8,128)(2,1)} %inverse_hbm.1, bf16[1,1024]{1,0:T(2,128)(2,1)} %targets_hbm.1, f32[256,256]{1,0:T(8,128)} %noise_hbm.1), custom_call_target="tpu_custom_call" | custom-call | tf_op jit(solution)/shard_map/samples/pallas_call | solution.py:358
  41.9 1.7 %copy.9 = f32[256,256]{1,0:T(8,128)} copy(f32[256,256]{1,0:T(8,128)} %samples.1) | data formatting | bytes 524288
